TPU v7x, 32 devices: a whole 2x2x4 slice. The times are simulated.
32 devices in a mesh: groups: 2 (over x), tm: 8 (over z, y), sector: 2 (over core).
Axes of the slice: x: 2, y: 2, z: 4, core: 2. Of those that a mesh axis runs over, the one named last changes fastest.
Arguments:
- context: bfloat16 [16, 2, 512, 256], P(('groups', 'tm'), 'sector'), parts along dimension 0, may hold values from -6 to 6
- depth_weight: float32 [16, 2, 16, 512], P(('groups', 'tm'), 'sector'), parts along dimension 0, may hold values from 0 to 1
- cell_ids: int32 [2, 16, 512], P('sector'), may hold values from 0 to 4095
- time_embed: bfloat16 [8, 256], replicated, may hold values from -3 to 3
- norm_gain: float32 [2, 2, 256], replicated, may hold values from 0.1 to 1.9
- w_qkv: bfloat16 [2, 256, 768], replicated, may hold values from -15 to 15
- w_out: bfloat16 [2, 256, 256], replicated, may hold values from -0.375 to 0.375
- w_up: bfloat16 [2, 256, 1024], replicated, may hold values from -0.375 to 0.375
- w_down: bfloat16 [2, 1024, 256], replicated, may hold values from -0.1875 to 0.1875
- conv_weight: bfloat16 [3, 3, 256, 256], replicated, may hold values from -0.125 to 0.125
Outputs:
- bev_out: bfloat16 [16, 64, 64, 256], P(('groups', 'tm'), 'sector'), parts along dimension 0
There are 2 independent parts, one for each index of `groups`. A program takes and returns all parts, laid end to end along the dimension named above; an argument that names none is the same for every part. Nothing has to cross between parts.
All inputs are finite; a program needn't handle non-finite values.
Results may differ from a plain program's by a relative error of at most 0.0079.
Values may be sent and summed in bfloat16 or wider, within the bound.
A program may use at most 128 MiB of HBM per device.

v0:
```python
import jax
import jax.numpy as jnp
from jax import lax
from jax.sharding import PartitionSpec as P

HEADS = 8
GRID = 64


def padded_2(cells, sides, width):
    for axis, dim in sides:
        count = lax.axis_size(axis)
        ends = count - 1
        head = lax.slice_in_dim(cells, 0, width, axis=dim)
        tail = lax.slice_in_dim(cells, cells.shape[dim] - width, cells.shape[dim], axis=dim)
        cells = jnp.concatenate(
            [
                lax.ppermute(tail, axis, [(i, (i + 1) % count) for i in range(ends)]),
                cells,
                lax.ppermute(head, axis, [((i + 1) % count, i) for i in range(ends)]),
            ],
            axis=dim,
        )
    return cells


def pool_local(context, depth_weight, cell_ids):
    cell_count = GRID * GRID
    block_cells = min(512, cell_count)
    cell_index = cell_ids[0]

    def one_frame(frame_inputs):
        features, weights = frame_inputs

        def one_block(first_cell):
            target = first_cell + lax.broadcasted_iota(jnp.int32, (block_cells, 1), 0)
            matches = cell_index[:, None, :] == target[None]
            matrix = jnp.sum(
                jnp.where(matches, weights[:, None, :], jnp.zeros_like(weights[:, None, :])), axis=0
            ).astype(jnp.bfloat16)
            return jnp.dot(matrix, features, preferred_element_type=jnp.float32).astype(
                jnp.bfloat16
            )

        starts = jnp.arange(cell_count // block_cells) * block_cells
        return lax.map(one_block, starts).reshape(cell_count, features.shape[-1])

    return lax.map(one_frame, (context[:, 0], depth_weight[:, 0]))


def normalize(values, gain):
    return values * lax.rsqrt(jnp.mean(values * values, axis=-1, keepdims=True) + 1e-05) * gain


def encode_stack(tokens, time_embed, norm_gain, w_qkv, w_out, w_up, w_down):
    frame_count, cell_count, channels = tokens.shape
    head_size = channels // HEADS
    query_frame = lax.broadcasted_iota(jnp.int32, (frame_count, frame_count), 0)
    key_frame = lax.broadcasted_iota(jnp.int32, (frame_count, frame_count), 1)
    allowed = key_frame <= query_frame
    stream = (tokens.astype(jnp.float32) + time_embed[:, None, :].astype(jnp.float32)).reshape(
        frame_count * cell_count, channels
    )
    for number in range(w_qkv.shape[0]):
        normed = normalize(stream, norm_gain[number, 0]).astype(jnp.bfloat16)
        projected = jnp.dot(normed, w_qkv[number], preferred_element_type=jnp.float32).astype(
            jnp.bfloat16
        )
        projected = projected.reshape(frame_count, cell_count, 3, HEADS, head_size)
        scores = jnp.einsum(
            "fchd,gchd->chfg",
            projected[:, :, 0],
            projected[:, :, 1],
            preferred_element_type=jnp.float32,
        ) * head_size ** (-0.5)
        scores = jnp.where(allowed, scores, -1e30)
        largest = jnp.max(scores, axis=-1, keepdims=True)
        raised = jnp.exp(scores - largest)
        soft_weights = (raised / jnp.sum(raised, axis=-1, keepdims=True)).astype(jnp.bfloat16)
        mixed = jnp.einsum(
            "chfg,gchd->fchd", soft_weights, projected[:, :, 2], preferred_element_type=jnp.float32
        ).astype(jnp.bfloat16)
        mixed = mixed.reshape(frame_count * cell_count, channels)
        stream = stream + jnp.dot(mixed, w_out[number], preferred_element_type=jnp.float32)
        normed_second = normalize(stream, norm_gain[number, 1]).astype(jnp.bfloat16)
        hidden_units = jax.nn.gelu(
            jnp.dot(normed_second, w_up[number], preferred_element_type=jnp.float32),
            approximate=True,
        ).astype(jnp.bfloat16)
        stream = stream + jnp.dot(hidden_units, w_down[number], preferred_element_type=jnp.float32)
    return stream.reshape(frame_count, cell_count, channels).astype(jnp.bfloat16)


def encode_return(tokens, weights):
    encoded = encode_stack(tokens, *weights)
    return lax.all_to_all(encoded, "tm", split_axis=0, concat_axis=1, tiled=True)


def body(
    context, depth_weight, cell_ids, time_embed, norm_gain, w_qkv, w_out, w_up, w_down, conv_weight
):
    partial_value = lax.optimization_barrier(pool_local(context, depth_weight, cell_ids))
    frames_dev, cell_count, channels = partial_value.shape
    tm_count = lax.axis_size("tm")
    band_cells = cell_count // lax.axis_size("sector")
    piece_cells = band_cells // tm_count
    weights = (time_embed, norm_gain, w_qkv, w_out, w_up, w_down)
    pooled = (
        lax.psum_scatter(partial_value, "sector", scatter_dimension=1, tiled=True)
        .astype(jnp.float32)
        .astype(jnp.bfloat16)
    )
    sectioned = pooled.reshape(frames_dev, tm_count, piece_cells, channels)
    received = lax.all_to_all(sectioned, "tm", split_axis=1, concat_axis=0, tiled=True)
    tokens = received.reshape(received.shape[0], received.shape[2], channels)
    returned = encode_return(tokens, weights)
    item_count = returned.shape[1] // tm_count
    result = returned.reshape(frames_dev, tm_count, item_count, channels)
    row_count = band_cells // GRID
    encoded = result.reshape(frames_dev, row_count, GRID, channels)
    padded = padded_2(encoded, (("sector", 1),), 1)
    padded = jnp.pad(padded, ((0, 0), (0, 0), (1, 1), (0, 0)))
    summed = encoded.astype(jnp.float32)
    for offset in range(3):
        row_strip = padded[:, offset : offset + row_count]
        stacked = jnp.concatenate(
            [row_strip[:, :, column : column + GRID] for column in range(3)], axis=-1
        )
        product = jnp.dot(
            stacked.reshape(frames_dev * row_count * GRID, 3 * channels),
            conv_weight[offset].reshape(3 * channels, channels),
            preferred_element_type=jnp.float32,
        )
        summed = summed + product.reshape(summed.shape)
    return summed.astype(jnp.bfloat16)


def solution(mesh):
    return jax.shard_map(
        body,
        mesh=mesh,
        in_specs=(
            P(("groups", "tm"), "sector", None, None),
            P(("groups", "tm"), "sector", None, None),
            P("sector", None, None),
            P(),
            P(),
            P(),
            P(),
            P(),
            P(),
            P(),
        ),
        out_specs=P(("groups", "tm"), "sector", None, None),
        check_vma=False,
    )
```

profile of v0, /device:TPU:0, one launch (start us, length us, event | category | flops | bytes accessed | tf_op | source)
XLA Modules:
  0.0 295.4 jit_solution(16586934135951967975)
XLA Ops:
  6.5 45.5 %while.17 = (s32[]{:T(128)}, bf16[8,512,256]{2,1,0:T(8,128)(2,1)}, s32[1,16,512]{2,1,0:T(8,128)}, s32[8]{0:T(128)S(1)}, f32[16,512]{1,0:T(8,128)}, /*index=5*/bf16[512,256]{1,0:T(8,128)(2,1)}, s32[]{:T(128)}) while((s32[]{:T(128)}, bf16[8,512,256]{2,1,0:T(8,128)(2,1)}, s32[1,16,512]{2,1,0:T(8,128)}, s32[8]{0:T(128)S(1)}, f32[16,512]{1,0:T(8,128)}, ...), condition=%wide.region_2.3_spmd, body=%wide.region_0.2_spmd.sunk | while | flops 146670080 | bytes 1643101 | solution.py:46
  52.0 12.5 %reduce-scatter.2.cloned.1.call-done = bf16[1,2048,256]{2,1,0:T(8,128)(2,1)} async-done(((bf16[1,4096,256]{2,1,0:T(8,128)(2,1)}), bf16[1,2048,256]{2,1,0:T(8,128)(2,1)}) %reduce-scatter.2.cloned.1.call-update) | async-done | bytes 1048592 | tf_op jit(solution)/shard_map/reduce_scatter | solution.py:109
  64.5 6.3 %all-to-all-start = ((bf16[1,8,256,256]{3,2,0,1:T(8,128)(2,1)}), bf16[1,8,256,256]{3,2,0,1:T(8,128)(2,1)S(1)}, u32[]{:S(2)}, u32[]{:S(2)}) async-start(bf16[1,8,256,256]{3,2,0,1:T(8,128)(2,1)} %bitcast.169), calls=%async_computation.1 | async-start | bytes 2097152 | tf_op jit(solution)/shard_map/all_to_all | solution.py:114
  70.9 26.1 %all-to-all-done = bf16[1,8,256,256]{3,2,0,1:T(8,128)(2,1)S(1)} async-done(((bf16[1,8,256,256]{3,2,0,1:T(8,128)(2,1)}), bf16[1,8,256,256]{3,2,0,1:T(8,128)(2,1)S(1)}, u32[]{:S(2)}, u32[]{:S(2)}) %all-to-all-start) | async-done | bytes 1048608 | tf_op jit(solution)/shard_map/all_to_all | solution.py:114
  106.1 7.2 %copy.70 = bf16[8,256,1,8,32]{4,0,3,1,2:T(8,128)(2,1)} copy(bf16[8,256,1,8,32]{1,0,4,3,2:T(8,128)(2,1)S(1)} %get-tuple-element.69) | data formatting | bytes 2097152
  113.3 7.2 %copy.71 = bf16[8,256,1,8,32]{4,0,3,1,2:T(8,128)(2,1)} copy(bf16[8,256,1,8,32]{1,0,4,3,2:T(8,128)(2,1)S(1)} %get-tuple-element.70) | data formatting | bytes 2097152
  120.5 9.0 %fusion.26 = f32[256,8,8,8]{2,3,1,0:T(8,128)} fusion(bf16[8,256,1,8,32]{4,0,3,1,2:T(8,128)(2,1)} %copy.71, bf16[8,256,1,8,32]{4,0,3,1,2:T(8,128)(2,1)} %copy.70), kind=kOutput, calls=%fused_computation.31 | convolution fusion | flops 8388608 | bytes 2621440 | tf_op jit(solution)/shard_map/fchd,gchd->chfg/dot_general | solution.py:70
  129.5 6.4 %copy.59 = f32[256,8,8,8]{0,3,2,1:T(8,128)S(1)} copy(f32[256,8,8,8]{2,3,1,0:T(8,128)} %fusion.26) | data formatting | bytes 1048576 | tf_op jit(solution)/shard_map/fchd,gchd->chfg/dot_general | solution.py:70
  136.9 6.4 %copy.60 = bf16[256,8,8,8]{3,2,1,0:T(8,128)(2,1)} copy(bf16[256,8,8,8]{0,3,2,1:T(8,128)(2,1)S(1)} %divide_convert_fusion.1) | data formatting | bytes 524288 | tf_op jit(solution)/shard_map/convert_element_type | solution.py:79
  143.4 7.4 %copy.69 = bf16[8,256,1,8,32]{4,0,3,1,2:T(8,128)(2,1)} copy(bf16[8,256,1,8,32]{1,0,4,3,2:T(8,128)(2,1)S(1)} %get-tuple-element.68) | data formatting | bytes 2097152
  150.7 7.8 %convert_bitcast_fusion.1 = bf16[8,256,8,32]{3,0,2,1:T(8,128)(2,1)} fusion(bf16[256,8,8,8]{3,2,1,0:T(8,128)(2,1)} %copy.60, bf16[8,256,1,8,32]{4,0,3,1,2:T(8,128)(2,1)} %copy.69), kind=kOutput, calls=%fused_computation.37 | convolution fusion | flops 8912896 | bytes 2359296 | tf_op jit(solution)/shard_map/chfg,gchd->fchd/dot_general | solution.py:80
  158.5 6.0 %copy.61 = bf16[8,256,8,32]{1,0,3,2:T(8,128)(2,1)S(1)} copy(bf16[8,256,8,32]{3,0,2,1:T(8,128)(2,1)} %convert_bitcast_fusion.1) | data formatting | bytes 2097152 | tf_op jit(solution)/shard_map/convert_element_type | solution.py:82
  166.2 5.9 %multiply_reduce_fusion.1 = (f32[2048]{0:T(1024)S(1)}, f32[2048,256]{1,0:T(8,128)}) fusion(f32[2048,256]{1,0:T(8,128)S(1)} %get-tuple-element.89, bf16[2,1024,256]{2,1,0:T(8,128)(2,1)} %param.20, f32[256]{0:T(256)S(1)} %bitcast.179, f32[2048]{0:T(1024)S(1)} %add_rsqrt_fusion.2, bf16[2,256,1024]{2,1,0:T(8,128)(2,1)} %param.19), kind=kOutput, calls=%fused_computation.83 | convolution fusion | flops 2169501696 | bytes 7357440 | tf_op jit(solution)/shard_map/dot_general | solution.py:90
  174.7 3.2 %copy.62 = bf16[2048,768]{0,1:T(8,128)(2,1)} copy(bf16[2048,768]{1,0:T(8,128)(2,1)S(1)} %convolution_convert_fusion.1) | data formatting | bytes 6291456 | tf_op jit(solution)/shard_map/convert_element_type | solution.py:66
  181.1 7.2 %copy.73 = bf16[8,256,1,8,32]{4,0,3,1,2:T(8,128)(2,1)} copy(bf16[8,256,1,8,32]{1,0,4,3,2:T(8,128)(2,1)S(1)} %get-tuple-element.66) | data formatting | bytes 2097152
  188.3 7.2 %copy.74 = bf16[8,256,1,8,32]{4,0,3,1,2:T(8,128)(2,1)} copy(bf16[8,256,1,8,32]{1,0,4,3,2:T(8,128)(2,1)S(1)} %get-tuple-element.67) | data formatting | bytes 2097152
  195.5 9.0 %fusion.21 = f32[256,8,8,8]{2,3,1,0:T(8,128)} fusion(bf16[8,256,1,8,32]{4,0,3,1,2:T(8,128)(2,1)} %copy.74, bf16[8,256,1,8,32]{4,0,3,1,2:T(8,128)(2,1)} %copy.73), kind=kOutput, calls=%fused_computation.26 | convolution fusion | flops 8388608 | bytes 2621440 | tf_op jit(solution)/shard_map/fchd,gchd->chfg/dot_general | solution.py:70
  204.5 6.4 %copy.66 = f32[256,8,8,8]{0,3,2,1:T(8,128)S(1)} copy(f32[256,8,8,8]{2,3,1,0:T(8,128)} %fusion.21) | data formatting | bytes 1048576 | tf_op jit(solution)/shard_map/fchd,gchd->chfg/dot_general | solution.py:70
  211.9 6.4 %copy.67 = bf16[256,8,8,8]{3,2,1,0:T(8,128)(2,1)} copy(bf16[256,8,8,8]{0,3,2,1:T(8,128)(2,1)S(1)} %divide_convert_fusion) | data formatting | bytes 524288 | tf_op jit(solution)/shard_map/convert_element_type | solution.py:79
  218.3 7.4 %copy.72 = bf16[8,256,1,8,32]{4,0,3,1,2:T(8,128)(2,1)} copy(bf16[8,256,1,8,32]{1,0,4,3,2:T(8,128)(2,1)S(1)} %get-tuple-element.65) | data formatting | bytes 2097152
  225.8 7.8 %convert_bitcast_fusion = bf16[8,256,8,32]{3,0,2,1:T(8,128)(2,1)} fusion(bf16[256,8,8,8]{3,2,1,0:T(8,128)(2,1)} %copy.67, bf16[8,256,1,8,32]{4,0,3,1,2:T(8,128)(2,1)} %copy.72), kind=kOutput, calls=%fused_computation.36 | convolution fusion | flops 8912896 | bytes 2359296 | tf_op jit(solution)/shard_map/chfg,gchd->fchd/dot_general | solution.py:80
  233.6 6.0 %copy.68 = bf16[8,256,8,32]{1,0,3,2:T(8,128)(2,1)S(1)} copy(bf16[8,256,8,32]{3,0,2,1:T(8,128)(2,1)} %convert_bitcast_fusion) | data formatting | bytes 2097152 | tf_op jit(solution)/shard_map/convert_element_type | solution.py:82
  241.8 5.6 %fusion.70 = bf16[2048,256]{1,0:T(8,128)(2,1)S(1)} fusion(f32[2048,256]{1,0:T(8,128)} %get-tuple-element.95, f32[256]{0:T(256)S(1)} %bitcast.178, f32[2048]{0:T(1024)S(1)} %add_rsqrt_fusion, bf16[2,1024,256]{2,1,0:T(8,128)(2,1)} %param.20, bf16[2,256,1024]{2,1,0:T(8,128)(2,1)} %param.19), kind=kOutput, calls=%fused_computation.72 | convolution fusion | flops 2168979456 | bytes 6300672 | tf_op jit(solution)/shard_map/dot_general | solution.py:90
  247.5 29.4 %all_to_all.8 = bf16[8,256,256]{2,1,0:T(8,128)(2,1)S(1)} all-to-all(bf16[8,256,256]{2,1,0:T(8,128)(2,1)S(1)} %bitcast.170), channel_id=1, replica_groups=mesh['groups'=2,'tm'=8,'sector'=2] {'tm'}, dimensions={0} | all-to-all | bytes 2097152 | tf_op jit(solution)/shard_map/all_to_all | solution.py:96
  (86 shorter events, 77.9 us)
Async XLA Ops:
  6.5 57.9 %reduce-scatter.2.cloned.1.call-start = ((), (), s32[]{:S(2)}) async-start(), calls=%async_computation.3 | async-start | bytes 3145728 | tf_op jit(solution)/shard_map/reduce_scatter | solution.py:109
  52.0 18.8 %copy-start.5 = (bf16[8,256]{1,0:T(8,128)(2,1)S(1)}, bf16[8,256]{1,0:T(8,128)(2,1)}, u32[]{:S(2)}) copy-start(bf16[8,256]{1,0:T(8,128)(2,1)} %param.15) | copy-start | bytes 12292
  52.0 18.9 %copy-start.6 = (f32[2,2,256]{2,1,0:T(2,128)S(1)}, f32[2,2,256]{2,1,0:T(2,128)}, u32[]{:S(2)}) copy-start(f32[2,2,256]{2,1,0:T(2,128)} %param.16) | copy-start | bytes 12292
  64.5 32.5 %all-to-all-start = ((bf16[1,8,256,256]{3,2,0,1:T(8,128)(2,1)}), bf16[1,8,256,256]{3,2,0,1:T(8,128)(2,1)S(1)}, u32[]{:S(2)}, u32[]{:S(2)}) async-start(bf16[1,8,256,256]{3,2,0,1:T(8,128)(2,1)} %bitcast.169), calls=%async_computation.1 | async-start | bytes 2097152 | tf_op jit(solution)/shard_map/all_to_all | solution.py:114
  97.0 1.0 copy-start
  158.5 6.3 %copy-start.1 = (bf16[1,8,256,256]{3,2,0,1:T(8,128)(2,1)S(1)}, bf16[1,8,256,256]{3,2,0,1:T(8,128)(2,1)}, u32[]{:S(2)}) copy-start(bf16[1,8,256,256]{3,2,0,1:T(8,128)(2,1)} %copy-done) | copy-start | bytes 3145732
  164.4 1.0 copy-start.4
  233.5 6.3 %copy-start.2 = (f32[2048,256]{1,0:T(8,128)S(1)}, f32[2048,256]{1,0:T(8,128)}, u32[]{:S(2)}) copy-start(f32[2048,256]{1,0:T(8,128)} %get-tuple-element.91) | copy-start | bytes 6291460
  241.8 37.6 %copy-start.3 = (bf16[3,3,256,256]{3,2,1,0:T(8,128)(2,1)S(1)}, bf16[3,3,256,256]{3,2,1,0:T(8,128)(2,1)}, u32[]{:S(2)}) copy-start(bf16[3,3,256,256]{3,2,1,0:T(8,128)(2,1)} %param.21) | copy-start | bytes 3538948
  276.8 2.7 collective-permute-start
  278.1 3.1 %collective-permute-start.1 = (bf16[1,1,64,256]{3,2,1,0:T(8,128)(2,1)S(1)}, bf16[1,1,64,256]{3,2,1,0:T(8,128)(2,1)S(1)}, u32[]{:S(2)}, u32[]{:S(2)}) collective-permute-start(bf16[1,1,64,256]{3,2,1,0:T(8,128)(2,1)S(1)} %get-tuple-element.81), channel_id=1, source_target_pairs={{1,0},{3,2},{5,4},{7,6},{9,8},{11,10},{13,12},{15,14},{17,16},{19,... | collective-permute-start | bytes 98312 | tf_op jit(solution)/shard_map/ppermute | solution.py:20
Sparse Core Ops, SparseCore 0:
  52.1 12.2 reduce-scatter.1
where the time goes:
time: 299 us; the launch traced here: 295 us
  local copies, waits for them, and re-layouts  101 us (34%)
  matrix products  73.3 us (25%)
  waiting for transfers between devices  40.3 us (13%)
  blocking collectives  29.4 us (10%)
  other arithmetic  28.7 us (10%)
  between operations  14 us (5%)
  starting transfers between devices  8.9 us (3%)
    unnamed x24, local copies, waits for them, and re-layouts  50.8 us
    all_to_all x1, blocking collectives, encode_return(): lax.all_to_all(encoded, 'tm', split_axis=0, concat_axis=1, tiled=True)  29.4 us
    all_to_all x1, waiting for transfers between devices, body(): lax.all_to_all(sectioned, 'tm', split_axis=1, concat_axis=0, tiled=True)  26.1 us
    reduce_sum x8, other arithmetic, one_block(): jnp.sum(jnp.where(matches, weights[:, None, :], jnp.zeros_like(weights[:,...  20 us
    dot_general x2, matrix products, encode_stack(): jnp.einsum('fchd,gchd->chfg', projected[:, :, 0], projected[:, :, 1], pre...  18 us
    dot_general x8, matrix products, one_block(): jnp.dot(matrix, features, preferred_element_type=jnp.float32)  15.7 us
    dot_general x2, matrix products, encode_stack(): jnp.einsum('chfg,gchd->fchd', soft_weights, projected[:, :, 2], preferred...  15.5 us
    convert_element_type x2, local copies, waits for them, and re-layouts, encode_stack(): (raised / jnp.sum(raised, axis=-1, keepdims=True)).astype(jnp.bfloat16)  12.8 us
  transfers between devices with their start and end apart: 4, of which 3 were waited for; matrix products, arithmetic and copies ran while one was open for 0% of the time, Pallas kernels for 0%

commit v1 on v0

v1 whole, which is shorter than its diff:
```python
import functools
import math

import jax
import jax.numpy as jnp
from jax import lax
from jax.experimental import pallas as pl
from jax.experimental.pallas import tpu as pltpu
from jax.sharding import PartitionSpec as P

HEADS = 8
GRID = 64
BF = jnp.bfloat16
F32 = jnp.float32
LANES16 = 16


def padded_2(cells, sides, width):
    for axis, dim in sides:
        count = lax.axis_size(axis)
        ends = count - 1
        head = lax.slice_in_dim(cells, 0, width, axis=dim)
        tail = lax.slice_in_dim(cells, cells.shape[dim] - width, cells.shape[dim], axis=dim)
        cells = jnp.concatenate(
            [
                lax.ppermute(tail, axis, [(i, (i + 1) % count) for i in range(ends)]),
                cells,
                lax.ppermute(head, axis, [((i + 1) % count, i) for i in range(ends)]),
            ],
            axis=dim,
        )
    return cells


def spread_rows(rows, out_ref):
    for d in range(rows.shape[0]):
        row = jnp.broadcast_to(rows[d : d + 1], (LANES16, rows.shape[1]))
        out_ref[d] = row.astype(BF)


def combine_bins(ids, weights, out_ref):
    rows = []
    for d in range(ids.shape[0]):
        same = jnp.where(ids == ids[d : d + 1], weights, 0.0)
        rows.append(jnp.sum(same, axis=0, keepdims=True))
    spread_rows(jnp.concatenate(rows, axis=0), out_ref)


def pool_block(ids, wide_ref, features, base, rows, loc_ref, matrix_ref):
    bins, pixels = ids.shape
    local = ids - base
    local = jnp.where((local >= 0) & (local < rows), local, -1).astype(F32)
    spread_rows(local, loc_ref)
    sub = min(64, rows)
    first = lax.broadcasted_iota(jnp.int32, (sub, pixels), 0).astype(F32)
    for part in range(rows // sub):
        cell = (first + float(part * sub)).astype(BF).reshape(sub // LANES16, LANES16, pixels)
        block = jnp.zeros(cell.shape, BF)
        for d in range(bins):
            block = jnp.where(cell == loc_ref[d][None], wide_ref[d][None], block)
        matrix_ref[part * sub : (part + 1) * sub] = block.reshape(sub, pixels)
    return jnp.dot(matrix_ref[...], features, preferred_element_type=F32).astype(BF)


def pool_kernel(rows, ids_ref, weight_ref, context_ref, out_ref, wide_ref, loc_ref, matrix_ref):
    sectors = ids_ref.shape[0]
    start = lax.axis_index("sector") * out_ref.shape[0]

    for s in range(sectors):
        combine_bins(ids_ref[s], weight_ref[s], wide_ref.at[s])

    @pl.loop(0, out_ref.shape[0] // rows)
    def _(step):
        total = None
        for s in range(sectors):
            part = pool_block(
                ids_ref[s],
                wide_ref.at[s],
                context_ref[s],
                start + step * rows,
                rows,
                loc_ref,
                matrix_ref,
            ).astype(F32)
            total = part if total is None else total + part
        out_ref[pl.ds(pl.multiple_of(step * rows, rows), rows)] = total.astype(BF)


def normalize(values, gain):
    return values * lax.rsqrt(jnp.mean(values * values, axis=-1, keepdims=True) + 1e-05) * gain


def encode_chunk(tokens, time_ref, gain_ref, qkv_ref, out_w_ref, up_ref, down_ref, head_sum, scratch):
    stream_ref, q_ref, k_ref, v_ref, mixed_ref = scratch
    frames, cells, channels = tokens.shape
    scale = (channels // HEADS) ** (-0.5) * math.log2(math.e)
    stream_ref[...] = tokens.astype(F32) + time_ref[...].astype(F32)[:, None, :]
    flat = (frames * cells, channels)

    def attend(f, count, masked):
        query = q_ref[f]
        product = (k_ref[0:count] * query[None]).reshape(count * cells, channels)
        high = product.astype(BF)
        low = (product - high.astype(F32)).astype(BF)
        scores = jnp.dot(high, head_sum, preferred_element_type=F32)
        scores = scores + jnp.dot(low, head_sum, preferred_element_type=F32)
        scores = scores.reshape(count, cells, channels)
        if masked:
            frame = lax.broadcasted_iota(jnp.int32, scores.shape, 0)
            scores = jnp.where(frame <= f, scores, -1e30)
        raised = jnp.exp2(scores - jnp.max(scores, axis=0, keepdims=True))
        mixed = jnp.sum(raised * v_ref[0:count], axis=0) / jnp.sum(raised, axis=0)
        mixed_ref[f] = mixed.astype(BF)

    def layer(l, carry):
        stream = stream_ref[...].reshape(flat)
        normed = normalize(stream, gain_ref[l, 0:1]).astype(BF)
        for i, ref in enumerate((q_ref, k_ref, v_ref)):
            part = jnp.dot(
                normed,
                qkv_ref[l, :, i * channels : (i + 1) * channels],
                preferred_element_type=F32,
            )
            part = part.astype(BF).astype(F32)
            ref[...] = (part * scale if i == 0 else part).reshape(ref.shape)
        if frames <= 8:
            for f in range(frames):
                attend(f, f + 1, False)
        else:
            lax.fori_loop(0, frames, lambda f, c: (attend(f, frames, True), c)[1], 0)
        stream = stream_ref[...].reshape(flat) + jnp.dot(
            mixed_ref[...].reshape(flat), out_w_ref[l], preferred_element_type=F32
        )
        normed = normalize(stream, gain_ref[l, 1:2]).astype(BF)
        hidden_width = up_ref.shape[2]
        step = min(256, hidden_width)
        for j in range(0, hidden_width, step):
            hidden = jnp.dot(normed, up_ref[l, :, j : j + step], preferred_element_type=F32)
            hidden = jax.nn.gelu(hidden, approximate=True).astype(BF)
            stream = stream + jnp.dot(
                hidden, down_ref[l, j : j + step, :], preferred_element_type=F32
            )
        stream_ref[...] = stream.reshape(stream_ref.shape)
        return carry

    lax.fori_loop(0, qkv_ref.shape[0], layer, 0)
    return stream_ref[...].astype(BF)


def head_matrix(channels):
    size = channels // HEADS
    row = lax.broadcasted_iota(jnp.int32, (channels, channels), 0) // size
    column = lax.broadcasted_iota(jnp.int32, (channels, channels), 1) // size
    return (row == column).astype(F32).astype(BF)


def encode_scratch(frames, cells, channels):
    shape = (frames, cells, channels)
    return [pltpu.VMEM(shape, F32)] * 4 + [pltpu.VMEM(shape, BF)]


def encode_kernel(tok_ref, time_ref, gain_ref, qkv_ref, ow_ref, up_ref, down_ref, out_ref, *scratch):
    channels = tok_ref.shape[-1]
    out_ref[...] = encode_chunk(
        tok_ref[...],
        time_ref,
        gain_ref,
        qkv_ref,
        ow_ref,
        up_ref,
        down_ref,
        head_matrix(channels),
        scratch,
    )


def body(
    context, depth_weight, cell_ids, time_embed, norm_gain, w_qkv, w_out, w_up, w_down, conv_weight
):
    tm_count = lax.axis_size("tm")
    frames_dev, _, pixels, channels = context.shape
    bins = cell_ids.shape[1]
    sectors = lax.axis_size("sector")
    band_cells = GRID * GRID // sectors
    piece_cells = band_cells // tm_count
    ids = lax.all_gather(cell_ids[0], "sector")
    weights = lax.all_gather(depth_weight[0, 0], "sector")
    features = lax.all_gather(context[0, 0], "sector")
    rows = min(256, band_cells)
    vmem = pl.BlockSpec(memory_space=pltpu.VMEM)
    pooled = pl.pallas_call(
        functools.partial(pool_kernel, rows),
        out_shape=jax.ShapeDtypeStruct((band_cells, channels), BF),
        in_specs=[vmem] * 3,
        out_specs=vmem,
        scratch_shapes=[
            pltpu.VMEM((sectors, bins, LANES16, pixels), BF),
            pltpu.VMEM((bins, LANES16, pixels), BF),
            pltpu.VMEM((rows, pixels), BF),
        ],
        compiler_params=pltpu.CompilerParams(vmem_limit_bytes=48 * 2**20),
    )(ids, weights, features)
    sectioned = pooled.reshape(frames_dev, tm_count, piece_cells, channels)
    received = lax.all_to_all(sectioned, "tm", split_axis=1, concat_axis=0, tiled=True)
    tokens = received.reshape(tm_count, piece_cells, channels)
    frames = tm_count
    chunk = math.gcd(64, piece_cells)
    block = pl.BlockSpec((frames, chunk, channels), lambda i: (0, i, 0))
    encoded = pl.pallas_call(
        encode_kernel,
        grid=(piece_cells // chunk,),
        out_shape=jax.ShapeDtypeStruct(tokens.shape, BF),
        in_specs=[block] + [vmem] * 6,
        out_specs=block,
        scratch_shapes=encode_scratch(frames, chunk, channels),
        compiler_params=pltpu.CompilerParams(vmem_limit_bytes=56 * 2**20),
    )(tokens, time_embed, norm_gain, w_qkv, w_out, w_up, w_down)
    returned = lax.all_to_all(encoded, "tm", split_axis=0, concat_axis=1, tiled=True)
    row_count = band_cells // GRID
    encoded = returned.reshape(frames_dev, row_count, GRID, channels)
    padded = padded_2(encoded, (("sector", 1),), 1)
    padded = jnp.pad(padded, ((0, 0), (0, 0), (1, 1), (0, 0)))
    summed = encoded.astype(jnp.float32)
    for offset in range(3):
        row_strip = padded[:, offset : offset + row_count]
        stacked = jnp.concatenate(
            [row_strip[:, :, column : column + GRID] for column in range(3)], axis=-1
        )
        product = jnp.dot(
            stacked.reshape(frames_dev * row_count * GRID, 3 * channels),
            conv_weight[offset].reshape(3 * channels, channels),
            preferred_element_type=jnp.float32,
        )
        summed = summed + product.reshape(summed.shape)
    return summed.astype(jnp.bfloat16)


def solution(mesh):
    return jax.shard_map(
        body,
        mesh=mesh,
        in_specs=(
            P(("groups", "tm"), "sector", None, None),
            P(("groups", "tm"), "sector", None, None),
            P("sector", None, None),
            P(),
            P(),
            P(),
            P(),
            P(),
            P(),
            P(),
        ),
        out_specs=P(("groups", "tm"), "sector", None, None),
        check_vma=False,
    )
```

time: 299 us -> 111 us (0.37); the launches traced: 295 us -> 111 us
  local copies, waits for them, and re-layouts: 101 us -> 1.18 us
  matrix products: 73.3 us -> 5.3 us
  blocking collectives: 29.4 us -> 68.9 us
  waiting for transfers between devices: 40.3 us -> 1.69 us
  Pallas kernels: 0 us -> 30.6 us
  other arithmetic: 28.7 us -> 0.68 us
  between operations: 14 us -> 0.08 us
  starting transfers between devices: 8.9 us -> 2.57 us
    dot_general x18 -> x0, matrix products: 68 us -> none  [the longest x2 18 us: encode_stack(): jnp.einsum('fchd,gchd->chfg', projected[:, :, 0], projected[:, :, 1], pre...]
    unnamed x24 -> x2, local copies, waits for them, and re-layouts: 50.8 us -> 0.01 us
    all_to_all x1 -> x2, blocking collectives: 29.4 us -> 62.4 us  [the longest x1 33.1 us: body(): lax.all_to_all(sectioned, 'tm', split_axis=1, concat_axis=0, tiled=True)]
    convert_element_type x6 -> x0, local copies, waits for them, and re-layouts: 31 us -> none  [the longest x2 12.8 us: encode_stack(): (raised / jnp.sum(raised, axis=-1, keepdims=True)).astype(jnp.bfloat16)]
    pallas_call x0 -> x2, Pallas kernels: none -> 30.6 us  [the longest x1 22.1 us: body(): pl.pallas_call(encode_kernel, grid=(piece_cells // chunk,), out_shape=jax...]
    all_to_all x1 -> x0, waiting for transfers between devices: 26.1 us -> none  [body(): lax.all_to_all(sectioned, 'tm', split_axis=1, concat_axis=0, tiled=True)]
    reduce_sum x9 -> x0, other arithmetic: 20.3 us -> none  [the longest x8 20 us: one_block(): jnp.sum(jnp.where(matches, weights[:, None, :], jnp.zeros_like(weights[:,...]
    dot_general x2 -> x0, local copies, waits for them, and re-layouts: 12.7 us -> none  [encode_stack(): jnp.einsum('fchd,gchd->chfg', projected[:, :, 0], projected[:, :, 1], pre...]
  transfers between devices with their start and end apart: 4 -> 2, of which waited for: 3 -> 1; matrix products, arithmetic and copies ran while one was open for 0% -> 0% of each run, Pallas kernels for 0% -> 0%
where the time goes in v1:
time: 111 us
  blocking collectives  68.9 us (62%)
  Pallas kernels  30.6 us (28%)
  matrix products  5.3 us (5%)
  starting transfers between devices  2.57 us (2%)
  waiting for transfers between devices  1.69 us (2%)
  local copies, waits for them, and re-layouts  1.18 us (1%)
    all_to_all x1, blocking collectives, body(): lax.all_to_all(sectioned, 'tm', split_axis=1, concat_axis=0, tiled=True)  33.1 us
    all_to_all x1, blocking collectives, body(): lax.all_to_all(encoded, 'tm', split_axis=0, concat_axis=1, tiled=True)  29.2 us
    pallas_call x1, Pallas kernels, body(): pl.pallas_call(encode_kernel, grid=(piece_cells // chunk,), out_shape=jax...  22.1 us
    pallas_call x1, Pallas kernels, body(): pl.pallas_call(functools.partial(pool_kernel, rows), out_shape=jax.ShapeD...  8.47 us
    dot_general x3, matrix products, body(): jnp.dot(stacked.reshape(frames_dev * row_count * GRID, 3 * channels), con...  5.3 us
    all_gather x1, blocking collectives, body(): features = lax.all_gather(context[0, 0], 'sector')  2.38 us
  transfers between devices with their start and end apart: 2, of which 1 were waited for; matrix products, arithmetic and copies ran while one was open for 0% of the time, Pallas kernels for 0%

profile of v1, /device:TPU:0, one launch (start us, length us, event | category | flops | bytes accessed | tf_op | source)
XLA Modules:
  0.0 111.0 jit_solution(10640226066980617688)
XLA Ops:
  0.0 2.2 %all-gather = f32[2,1,16,512]{3,2,1,0:T(8,128)S(1)} all-gather(f32[1,1,16,512]{3,2,1,0:T(8,128)} %param.11), channel_id=2, replica_groups=mesh['groups'=2,'tm'=8,'sector'=2] {'sector'}, dimensions={0}, use_global_device_ids=true | all-gather | bytes 98304 | tf_op jit(solution)/shard_map/all_gather | solution.py:187
  2.2 2.1 %all_gather.9.ids_ref = s32[2,16,512]{2,1,0:T(8,128)S(1)} all-gather(s32[1,16,512]{2,1,0:T(8,128)} %param.12), channel_id=1, replica_groups=mesh['groups'=2,'tm'=8,'sector'=2] {'sector'}, dimensions={0}, use_global_device_ids=true | all-gather | bytes 98304 | tf_op jit(solution)/shard_map/all_gather | solution.py:186
  4.2 2.4 %all-gather.1 = bf16[2,1,512,256]{3,2,1,0:T(8,128)(2,1)S(1)} all-gather(bf16[1,1,512,256]{3,2,1,0:T(8,128)(2,1)} %param.10), channel_id=3, replica_groups=mesh['groups'=2,'tm'=8,'sector'=2] {'sector'}, dimensions={0}, use_global_device_ids=true | all-gather | bytes 786432 | tf_op jit(solution)/shard_map/all_gather | solution.py:188
  6.6 8.5 %shard_map.100 = bf16[2048,256]{1,0:T(8,128)(2,1)S(1)} custom-call(s32[2,16,512]{2,1,0:T(8,128)S(1)} %all_gather.9.ids_ref, f32[2,16,512]{2,1,0:T(8,128)S(1)} %bitcast.38, bf16[2,512,256]{2,1,0:T(8,128)(2,1)S(1)} %bitcast.37), custom_call_target="tpu_custom_call" | custom-call | tf_op jit(solution)/shard_map/pallas_call | solution.py:191
  15.1 33.1 %all_to_all.8 = bf16[1,8,256,256]{3,2,0,1:T(8,128)(2,1)} all-to-all(bf16[1,8,256,256]{3,2,0,1:T(8,128)(2,1)S(1)} %bitcast.36), channel_id=1, replica_groups=mesh['groups'=2,'tm'=8,'sector'=2] {'tm'}, dimensions={1} | all-to-all | bytes 2097152 | tf_op jit(solution)/shard_map/all_to_all | solution.py:204
  48.2 22.1 %shard_map.101 = bf16[8,256,256]{2,1,0:T(8,128)(2,1)} custom-call(bf16[8,256,256]{2,1,0:T(8,128)(2,1)} %bitcast.45, bf16[8,256]{1,0:T(8,128)(2,1)} %time_ref.1, f32[2,2,256]{2,1,0:T(2,128)} %gain_ref.1, bf16[2,256,768]{2,1,0:T(8,128)(2,1)} %qkv_ref.1, bf16[2,256,256]{2,1,0:T(8,128)(2,1)} %ow_ref.1, bf16[2,256,1024]{2,1,0:T(8,128)(2,1)} %up_ref.1, ...), custom_call_target="tpu_custom_call" | custom-call | tf_op jit(solution)/shard_map/pallas_call | solution.py:209
  70.3 0.0 copy-start
  70.3 29.2 %all_to_all.9 = bf16[8,256,256]{2,1,0:T(8,128)(2,1)S(1)} all-to-all(bf16[8,256,256]{2,1,0:T(8,128)(2,1)} %shard_map.101), channel_id=1, replica_groups=mesh['groups'=2,'tm'=8,'sector'=2] {'tm'}, dimensions={0} | all-to-all | bytes 2097152 | tf_op jit(solution)/shard_map/all_to_all | solution.py:218
  99.5 1.3 %collective-permute-start = (bf16[1,1,64,256]{3,2,1,0:T(8,128)(2,1)S(1)}, bf16[1,1,64,256]{3,2,1,0:T(8,128)(2,1)S(1)}, u32[]{:S(2)}, u32[]{:S(2)}) collective-permute-start(bf16[1,1,64,256]{3,2,1,0:T(8,128)(2,1)S(1)} %get-tuple-element.14), channel_id=1, source_target_pairs={{0,1},{2,3},{4,5},{6,7},{8,9},{10,11},{12,13},{14,15},{16,17},{18,... | collective-permute-start | bytes 98312 | tf_op jit(solution)/shard_map/ppermute | solution.py:26
  100.8 1.3 %collective-permute-start.1 = (bf16[1,1,64,256]{3,2,1,0:T(8,128)(2,1)S(1)}, bf16[1,1,64,256]{3,2,1,0:T(8,128)(2,1)S(1)}, u32[]{:S(2)}, u32[]{:S(2)}) collective-permute-start(bf16[1,1,64,256]{3,2,1,0:T(8,128)(2,1)S(1)} %get-tuple-element.15), channel_id=1, source_target_pairs={{1,0},{3,2},{5,4},{7,6},{9,8},{11,10},{13,12},{15,14},{17,16},{19,... | collective-permute-start | bytes 98312 | tf_op jit(solution)/shard_map/ppermute | solution.py:28
  102.1 0.0 copy-done
  102.1 0.1 fusion.39
  102.2 0.0 collective-permute-done
  102.2 1.7 %collective-permute-done.1 = bf16[1,1,64,256]{3,2,1,0:T(8,128)(2,1)S(1)} collective-permute-done((bf16[1,1,64,256]{3,2,1,0:T(8,128)(2,1)S(1)}, bf16[1,1,64,256]{3,2,1,0:T(8,128)(2,1)S(1)}, u32[]{:S(2)}, u32[]{:S(2)}) %collective-permute-start.1) | collective-permute-done | bytes 32800 | tf_op jit(solution)/shard_map/ppermute | solution.py:28
  103.9 0.7 fusion.34
  104.6 1.1 fusion.38
  105.7 1.6 %fusion.14 = f32[32,64,256]{2,1,0:T(8,128)S(1)} fusion(bf16[768,256,1]{1,0,2:T(8,128)(2,1)S(1)} %bitcast.48, bf16[1,32,64,256]{3,2,1,0:T(8,128)(2,1)S(1)} %get-tuple-element.7, bf16[1,32,64,256]{3,2,1,0:T(8,128)(2,1)S(1)} %bitcast.41, bf16[1,32,64,256]{3,2,1,0:T(8,128)(2,1)S(1)} %get-tuple-element.8), kind=kOutput, calls=%fused_computation.17 | convolution fusion | flops 814743552 | bytes 5636096 | tf_op jit(solution)/shard_map/dot_general | solution.py:229
  107.3 1.6 %fusion.9 = f32[32,64,256]{2,1,0:T(8,128)S(1)} fusion(bf16[768,256,1]{1,0,2:T(8,128)(2,1)S(1)} %bitcast.47, bf16[1,32,64,256]{3,2,1,0:T(8,128)(2,1)S(1)} %bitcast.42, bf16[1,1,64,256]{3,2,1,0:T(8,128)(2,1)S(1)} %collective-permute-done, bf16[1,32,64,256]{3,2,1,0:T(8,128)(2,1)S(1)} %get-tuple-element.9, bf16[1,32,64,256]{3,2,1,0:T(8,128)(2,1)S(1)} %get-tuple-element.5), kind=kOutput, calls=%fused_computation.12 | convolution fusion | flops 817889280 | bytes 5668864 | tf_op jit(solution)/shard_map/dot_general | solution.py:229
  108.9 2.1 %fusion.30 = bf16[1,32,64,256]{3,2,1,0:T(8,128)(2,1)} fusion(bf16[768,256,1]{1,0,2:T(8,128)(2,1)S(1)} %bitcast.46, bf16[1,1,64,256]{3,2,1,0:T(8,128)(2,1)S(1)} %collective-permute-done.1, bf16[1,32,64,256]{3,2,1,0:T(8,128)(2,1)S(1)} %bitcast.43, bf16[1,32,64,256]{3,2,1,0:T(8,128)(2,1)S(1)} %get-tuple-element.10, ...), kind=kOutput, calls=%fused_computation.32 | convolution fusion | flops 820510720 | bytes 9863168 | tf_op jit(solution)/shard_map/dot_general | solution.py:229
  (1 shorter events, 0.0 us)
Async XLA Ops:
  70.3 31.8 %copy-start = (bf16[3,3,256,256]{3,2,1,0:T(8,128)(2,1)S(1)}, bf16[3,3,256,256]{3,2,1,0:T(8,128)(2,1)}, u32[]{:S(2)}) copy-start(bf16[3,3,256,256]{3,2,1,0:T(8,128)(2,1)} %param.19) | copy-start | bytes 3538948
  99.5 2.7 %collective-permute-start = (bf16[1,1,64,256]{3,2,1,0:T(8,128)(2,1)S(1)}, bf16[1,1,64,256]{3,2,1,0:T(8,128)(2,1)S(1)}, u32[]{:S(2)}, u32[]{:S(2)}) collective-permute-start(bf16[1,1,64,256]{3,2,1,0:T(8,128)(2,1)S(1)} %get-tuple-element.14), channel_id=1, source_target_pairs={{0,1},{2,3},{4,5},{6,7},{8,9},{10,11},{12,13},{14,15},{16,17},{18,... | collective-permute-start | bytes 98312 | tf_op jit(solution)/shard_map/ppermute | solution.py:26
  100.8 3.1 %collective-permute-start.1 = (bf16[1,1,64,256]{3,2,1,0:T(8,128)(2,1)S(1)}, bf16[1,1,64,256]{3,2,1,0:T(8,128)(2,1)S(1)}, u32[]{:S(2)}, u32[]{:S(2)}) collective-permute-start(bf16[1,1,64,256]{3,2,1,0:T(8,128)(2,1)S(1)} %get-tuple-element.15), channel_id=1, source_target_pairs={{1,0},{3,2},{5,4},{7,6},{9,8},{11,10},{13,12},{15,14},{17,16},{19,... | collective-permute-start | bytes 98312 | tf_op jit(solution)/shard_map/ppermute | solution.py:28

commit v2 on v1

--- a/solution.py
+++ b/solution.py
@@ -13,23 +13,6 @@
 BF = jnp.bfloat16
 F32 = jnp.float32
 LANES16 = 16
-
-
-def padded_2(cells, sides, width):
-    for axis, dim in sides:
-        count = lax.axis_size(axis)
-        ends = count - 1
-        head = lax.slice_in_dim(cells, 0, width, axis=dim)
-        tail = lax.slice_in_dim(cells, cells.shape[dim] - width, cells.shape[dim], axis=dim)
-        cells = jnp.concatenate(
-            [
-                lax.ppermute(tail, axis, [(i, (i + 1) % count) for i in range(ends)]),
-                cells,
-                lax.ppermute(head, axis, [((i + 1) % count, i) for i in range(ends)]),
-            ],
-            axis=dim,
-        )
-    return cells
 
 
 def spread_rows(rows, out_ref):
@@ -60,30 +43,6 @@
             block = jnp.where(cell == loc_ref[d][None], wide_ref[d][None], block)
         matrix_ref[part * sub : (part + 1) * sub] = block.reshape(sub, pixels)
     return jnp.dot(matrix_ref[...], features, preferred_element_type=F32).astype(BF)
-
-
-def pool_kernel(rows, ids_ref, weight_ref, context_ref, out_ref, wide_ref, loc_ref, matrix_ref):
-    sectors = ids_ref.shape[0]
-    start = lax.axis_index("sector") * out_ref.shape[0]
-
-    for s in range(sectors):
-        combine_bins(ids_ref[s], weight_ref[s], wide_ref.at[s])
-
-    @pl.loop(0, out_ref.shape[0] // rows)
-    def _(step):
-        total = None
-        for s in range(sectors):
-            part = pool_block(
-                ids_ref[s],
-                wide_ref.at[s],
-                context_ref[s],
-                start + step * rows,
-                rows,
-                loc_ref,
-                matrix_ref,
-            ).astype(F32)
-            total = part if total is None else total + part
-        out_ref[pl.ds(pl.multiple_of(step * rows, rows), rows)] = total.astype(BF)
 
 
 def normalize(values, gain):
@@ -159,80 +118,351 @@
     return [pltpu.VMEM(shape, F32)] * 4 + [pltpu.VMEM(shape, BF)]
 
 
-def encode_kernel(tok_ref, time_ref, gain_ref, qkv_ref, ow_ref, up_ref, down_ref, out_ref, *scratch):
-    channels = tok_ref.shape[-1]
-    out_ref[...] = encode_chunk(
-        tok_ref[...],
-        time_ref,
-        gain_ref,
-        qkv_ref,
-        ow_ref,
-        up_ref,
-        down_ref,
-        head_matrix(channels),
-        scratch,
-    )
+def conv_rows(x_ref, cat_ref, first, count):
+    channels = x_ref.shape[1]
+    centre = x_ref[pl.ds(first, count)]
+    values = centre.astype(F32)
+    column = lax.broadcasted_iota(jnp.int32, values.shape, 0) % GRID
+    left = jnp.where(column == 0, 0.0, pltpu.roll(values, 1, 0)).astype(BF)
+    right = jnp.where(column == GRID - 1, 0.0, pltpu.roll(values, count - 1, 0)).astype(BF)
+    cat_ref[pl.ds(first, count), 0:channels] = left
+    cat_ref[pl.ds(first, count), channels : 2 * channels] = centre
+    cat_ref[pl.ds(first, count), 2 * channels :] = right
+
+
+def fused_kernel(
+    tm_count,
+    sectors,
+    piece,
+    chunk,
+    context_ref,
+    weight_ref,
+    ids_ref,
+    time_ref,
+    gain_ref,
+    qkv_hbm,
+    ow_hbm,
+    up_hbm,
+    down_hbm,
+    conv_hbm,
+    result_ref,
+    qkv_ref,
+    ow_ref,
+    up_ref,
+    down_ref,
+    conv_ref,
+    far_context,
+    far_weight,
+    far_ids,
+    wide_ref,
+    perm_ref,
+    loc_ref,
+    matrix_ref,
+    send_ref,
+    recv_ref,
+    enc_ref,
+    x_ref,
+    cat_ref,
+    load_sem,
+    sector_send,
+    sector_recv,
+    go_send,
+    go_recv,
+    back_send,
+    back_recv,
+    edge_send,
+    edge_recv,
+    *scratch,
+):
+    me = lax.axis_index("tm")
+    sector = lax.axis_index("sector")
+    pixels, channels = context_ref.shape
+    chunks = piece // chunk
+    band = tm_count * piece
+    bins = ids_ref.shape[0]
+
+    loads = []
+    for i, (a, b) in enumerate(
+        (
+            (qkv_hbm, qkv_ref),
+            (ow_hbm, ow_ref),
+            (up_hbm, up_ref),
+            (down_hbm, down_ref),
+            (conv_hbm, conv_ref),
+        )
+    ):
+        loads.append(pltpu.make_async_copy(a, b, load_sem.at[i]))
+        loads[-1].start()
+
+    barrier = pltpu.get_barrier_semaphore()
+
+    @pl.loop(1, tm_count)
+    def _(o):
+        pl.semaphore_signal(
+            barrier,
+            inc=1,
+            device_id={"tm": lax.rem(me + o, tm_count)},
+            device_id_type=pl.DeviceIdType.MESH,
+        )
+
+    for o in range(1, sectors):
+        pl.semaphore_signal(
+            barrier,
+            inc=1,
+            device_id={"sector": lax.rem(sector + o, sectors)},
+            device_id_type=pl.DeviceIdType.MESH,
+        )
+    pl.semaphore_wait(barrier, tm_count - 1 + sectors - 1)
+
+    swaps = []
+    for o in range(1, sectors):
+        for i, (a, b) in enumerate(
+            ((ids_ref, far_ids), (weight_ref, far_weight), (context_ref, far_context))
+        ):
+            swaps.append(
+                pltpu.make_async_remote_copy(
+                    src_ref=a,
+                    dst_ref=b.at[o - 1],
+                    send_sem=sector_send.at[o - 1, i],
+                    recv_sem=sector_recv.at[o - 1, i],
+                    device_id={"sector": lax.rem(sector + o, sectors)},
+                    device_id_type=pl.DeviceIdType.MESH,
+                )
+            )
+            swaps[-1].start()
+
+    def prepare(s, ids, weights):
+        combine_bins(ids, weights, wide_ref.at[s])
+        local = ids - sector * band
+        inside = (local >= 0) & (local < band)
+        local = jnp.where(inside, local, 0)
+        owner, rest = local // piece, local % piece
+        place = ((rest // chunk) * tm_count + owner) * chunk + rest % chunk
+        perm_ref[s] = jnp.where(inside, place, -1)
+
+    prepare(0, ids_ref[...], weight_ref[...])
+    for o in range(1, sectors):
+        for copy in swaps[3 * (o - 1) : 3 * o]:
+            copy.wait()
+        prepare(o, far_ids[o - 1], far_weight[o - 1])
+
+    rows = matrix_ref.shape[0]
+    blocks = tm_count * chunk // rows
+    per = rows // chunk
+
+    def go_copy(c, target, source):
+        return pltpu.make_async_remote_copy(
+            src_ref=send_ref.at[c * tm_count + target],
+            dst_ref=recv_ref.at[c, source],
+            send_sem=go_send.at[c, target],
+            recv_sem=go_recv.at[c, source],
+            device_id={"tm": target},
+            device_id_type=pl.DeviceIdType.MESH,
+        )
+
+    def back_copy(c, target, source):
+        return pltpu.make_async_remote_copy(
+            src_ref=enc_ref.at[c, target],
+            dst_ref=x_ref.at[pl.ds(pl.multiple_of(GRID + source * piece + c * chunk, 16), chunk)],
+            send_sem=back_send.at[c, target],
+            recv_sem=back_recv.at[c, source],
+            device_id={"tm": target},
+            device_id_type=pl.DeviceIdType.MESH,
+        )
+
+    @pl.loop(0, chunks)
+    def _(c):
+        @pl.loop(0, blocks)
+        def _(b):
+            step = c * blocks + b
+            total = None
+            for s in range(sectors):
+                features = context_ref[...] if s == 0 else far_context[s - 1]
+                part = pool_block(
+                    perm_ref[s], wide_ref.at[s], features, step * rows, rows, loc_ref, matrix_ref
+                ).astype(F32)
+                total = part if total is None else total + part
+            send_ref[pl.ds(step * per, per)] = total.astype(BF).reshape(per, chunk, channels)
+
+        @pl.loop(1, tm_count)
+        def _(o):
+            go_copy(c, lax.rem(me + o, tm_count), me).start()
+
+        recv_ref[c, me] = send_ref[c * tm_count + me]
+
+    for load in loads:
+        load.wait()
+    head_sum = head_matrix(channels)
+
+    @pl.loop(0, chunks)
+    def _(c):
+        @pl.loop(1, tm_count)
+        def _(o):
+            go_copy(c, me, lax.rem(me + tm_count - o, tm_count)).wait_recv()
+
+        enc_ref[c] = encode_chunk(
+            recv_ref[c],
+            time_ref,
+            gain_ref,
+            qkv_ref,
+            ow_ref,
+            up_ref,
+            down_ref,
+            head_sum,
+            scratch,
+        )
+
+        @pl.loop(1, tm_count)
+        def _(o):
+            back_copy(c, lax.rem(me + o, tm_count), me).start()
+
+        here = pl.multiple_of(GRID + me * piece + c * chunk, 16)
+        x_ref[pl.ds(here, chunk)] = enc_ref[c, me]
+
+    @pl.loop(0, chunks)
+    def _(c):
+        @pl.loop(1, tm_count)
+        def _(o):
+            back_copy(c, me, lax.rem(me + tm_count - o, tm_count)).wait_recv()
+
+    def edge_copy(way):
+        return pltpu.make_async_remote_copy(
+            src_ref=x_ref.at[pl.ds(band if way == 0 else GRID, GRID)],
+            dst_ref=x_ref.at[pl.ds(0 if way == 0 else band + GRID, GRID)],
+            send_sem=edge_send.at[way],
+            recv_sem=edge_recv.at[way],
+            device_id={"sector": lax.rem(sector + (1 if way == 0 else sectors - 1), sectors)},
+            device_id_type=pl.DeviceIdType.MESH,
+        )
+
+    blank = jnp.zeros((GRID, channels), BF)
+
+    @pl.when(sector < sectors - 1)
+    def _():
+        edge_copy(0).start()
+
+    @pl.when(sector > 0)
+    def _():
+        edge_copy(1).start()
+
+    @pl.when(sector == 0)
+    def _():
+        x_ref[0:GRID] = blank
+
+    @pl.when(sector == sectors - 1)
+    def _():
+        x_ref[band + GRID : band + 2 * GRID] = blank
+
+    tall = math.gcd(band, 8 * GRID)
+
+    @pl.loop(0, band // tall)
+    def _(i):
+        conv_rows(x_ref, cat_ref, pl.multiple_of(GRID + i * tall, GRID), tall)
+
+    @pl.when(sector > 0)
+    def _():
+        edge_copy(0).wait_recv()
+
+    @pl.when(sector < sectors - 1)
+    def _():
+        edge_copy(1).wait_recv()
+
+    conv_rows(x_ref, cat_ref, 0, GRID)
+    conv_rows(x_ref, cat_ref, band + GRID, GRID)
+
+    @pl.loop(0, band // tall)
+    def _(i):
+        first = pl.multiple_of(i * tall, GRID)
+        total = x_ref[pl.ds(pl.multiple_of(first + GRID, GRID), tall)].astype(F32)
+        for r in range(3):
+            strip = cat_ref[pl.ds(pl.multiple_of(first + r * GRID, GRID), tall)]
+            total = total + jnp.dot(strip, conv_ref[r], preferred_element_type=F32)
+        result_ref[pl.ds(first, tall)] = total.astype(BF)
+
+    @pl.when(sector < sectors - 1)
+    def _():
+        edge_copy(0).wait_send()
+
+    @pl.when(sector > 0)
+    def _():
+        edge_copy(1).wait_send()
+
+    @pl.loop(0, chunks)
+    def _(c):
+        @pl.loop(1, tm_count)
+        def _(o):
+            target = lax.rem(me + o, tm_count)
+            go_copy(c, target, me).wait_send()
+            back_copy(c, target, me).wait_send()
 
 
 def body(
     context, depth_weight, cell_ids, time_embed, norm_gain, w_qkv, w_out, w_up, w_down, conv_weight
 ):
     tm_count = lax.axis_size("tm")
-    frames_dev, _, pixels, channels = context.shape
+    sectors = lax.axis_size("sector")
+    pixels, channels = context.shape[2:]
     bins = cell_ids.shape[1]
-    sectors = lax.axis_size("sector")
-    band_cells = GRID * GRID // sectors
-    piece_cells = band_cells // tm_count
-    ids = lax.all_gather(cell_ids[0], "sector")
-    weights = lax.all_gather(depth_weight[0, 0], "sector")
-    features = lax.all_gather(context[0, 0], "sector")
-    rows = min(256, band_cells)
+    band = GRID * GRID // sectors
+    piece = band // tm_count
+    chunk = math.gcd(64, piece)
+    chunks = piece // chunk
+    rows = math.gcd(256, tm_count * chunk)
+    conv_flat = conv_weight.reshape(3, 3 * channels, channels)
     vmem = pl.BlockSpec(memory_space=pltpu.VMEM)
-    pooled = pl.pallas_call(
-        functools.partial(pool_kernel, rows),
-        out_shape=jax.ShapeDtypeStruct((band_cells, channels), BF),
-        in_specs=[vmem] * 3,
+    anywhere = pl.BlockSpec(memory_space=pl.ANY)
+    dma = pltpu.SemaphoreType.DMA
+    far = sectors - 1
+    result = pl.pallas_call(
+        functools.partial(fused_kernel, tm_count, sectors, piece, chunk),
+        out_shape=jax.ShapeDtypeStruct((band, channels), BF),
+        in_specs=[vmem] * 5 + [anywhere] * 5,
         out_specs=vmem,
         scratch_shapes=[
+            pltpu.VMEM(w_qkv.shape, BF),
+            pltpu.VMEM(w_out.shape, BF),
+            pltpu.VMEM(w_up.shape, BF),
+            pltpu.VMEM(w_down.shape, BF),
+            pltpu.VMEM(conv_flat.shape, BF),
+            pltpu.VMEM((far, pixels, channels), BF),
+            pltpu.VMEM((far, bins, pixels), F32),
+            pltpu.VMEM((far, bins, pixels), jnp.int32),
             pltpu.VMEM((sectors, bins, LANES16, pixels), BF),
+            pltpu.VMEM((sectors, bins, pixels), jnp.int32),
             pltpu.VMEM((bins, LANES16, pixels), BF),
             pltpu.VMEM((rows, pixels), BF),
-        ],
-        compiler_params=pltpu.CompilerParams(vmem_limit_bytes=48 * 2**20),
-    )(ids, weights, features)
-    sectioned = pooled.reshape(frames_dev, tm_count, piece_cells, channels)
-    received = lax.all_to_all(sectioned, "tm", split_axis=1, concat_axis=0, tiled=True)
-    tokens = received.reshape(tm_count, piece_cells, channels)
-    frames = tm_count
-    chunk = math.gcd(64, piece_cells)
-    block = pl.BlockSpec((frames, chunk, channels), lambda i: (0, i, 0))
-    encoded = pl.pallas_call(
-        encode_kernel,
-        grid=(piece_cells // chunk,),
-        out_shape=jax.ShapeDtypeStruct(tokens.shape, BF),
-        in_specs=[block] + [vmem] * 6,
-        out_specs=block,
-        scratch_shapes=encode_scratch(frames, chunk, channels),
-        compiler_params=pltpu.CompilerParams(vmem_limit_bytes=56 * 2**20),
-    )(tokens, time_embed, norm_gain, w_qkv, w_out, w_up, w_down)
-    returned = lax.all_to_all(encoded, "tm", split_axis=0, concat_axis=1, tiled=True)
-    row_count = band_cells // GRID
-    encoded = returned.reshape(frames_dev, row_count, GRID, channels)
-    padded = padded_2(encoded, (("sector", 1),), 1)
-    padded = jnp.pad(padded, ((0, 0), (0, 0), (1, 1), (0, 0)))
-    summed = encoded.astype(jnp.float32)
-    for offset in range(3):
-        row_strip = padded[:, offset : offset + row_count]
-        stacked = jnp.concatenate(
-            [row_strip[:, :, column : column + GRID] for column in range(3)], axis=-1
-        )
-        product = jnp.dot(
-            stacked.reshape(frames_dev * row_count * GRID, 3 * channels),
-            conv_weight[offset].reshape(3 * channels, channels),
-            preferred_element_type=jnp.float32,
-        )
-        summed = summed + product.reshape(summed.shape)
-    return summed.astype(jnp.bfloat16)
+            pltpu.VMEM((chunks * tm_count, chunk, channels), BF),
+            pltpu.VMEM((chunks, tm_count, chunk, channels), BF),
+            pltpu.VMEM((chunks, tm_count, chunk, channels), BF),
+            pltpu.VMEM((band + 2 * GRID, channels), BF),
+            pltpu.VMEM((band + 2 * GRID, 3 * channels), BF),
+            dma((5,)),
+            dma((far, 3)),
+            dma((far, 3)),
+            dma((chunks, tm_count)),
+            dma((chunks, tm_count)),
+            dma((chunks, tm_count)),
+            dma((chunks, tm_count)),
+            dma((2,)),
+            dma((2,)),
+        ]
+        + encode_scratch(tm_count, chunk, channels),
+        compiler_params=pltpu.CompilerParams(
+            collective_id=0, has_side_effects=True, vmem_limit_bytes=60 * 2**20
+        ),
+    )(
+        context[0, 0],
+        depth_weight[0, 0],
+        cell_ids[0],
+        time_embed,
+        norm_gain,
+        w_qkv,
+        w_out,
+        w_up,
+        w_down,
+        conv_flat,
+    )
+    return result.reshape(1, band // GRID, GRID, channels)
 
 
 def solution(mesh):

time: 111 us -> 64.5 us (0.58)
  blocking collectives: 68.9 us -> 0 us
  Pallas kernels: 30.6 us -> 61.8 us
  matrix products: 5.3 us -> 0 us
  starting transfers between devices: 2.57 us -> 0 us
  waiting for transfers between devices: 1.69 us -> 0 us
  local copies, waits for them, and re-layouts: 1.18 us -> 2.3 us
    all_to_all x2 -> x0, blocking collectives: 62.4 us -> none  [the longest x1 33.1 us: body(): lax.all_to_all(sectioned, 'tm', split_axis=1, concat_axis=0, tiled=True)]
    pallas_call x2 -> x1, Pallas kernels: 30.6 us -> 61.8 us  [body(): pl.pallas_call(functools.partial(fused_kernel, tm_count, sectors, piece,...]
    all_gather x3 -> x0, blocking collectives: 6.59 us -> none  [the longest x1 2.38 us: body(): features = lax.all_gather(context[0, 0], 'sector')]
    dot_general x3 -> x0, matrix products: 5.3 us -> none  [body(): jnp.dot(stacked.reshape(frames_dev * row_count * GRID, 3 * channels), con...]
    ppermute x2 -> x0, starting transfers between devices: 2.57 us -> none  [the longest x1 1.29 us: padded_2(): lax.ppermute(head, axis, [((i + 1) % count, i) for i in range(ends)])]
    unnamed x2 -> x1, local copies, waits for them, and re-layouts: 0.01 us -> 2.3 us
    ppermute x2 -> x0, waiting for transfers between devices: 1.69 us -> none  [the longest x1 1.69 us: padded_2(): lax.ppermute(head, axis, [((i + 1) % count, i) for i in range(ends)])]
    slice x3 -> x0, local copies, waits for them, and re-layouts: 1.18 us -> none  [the longest x1 1.09 us: body(): row_strip[:, :, column:column + GRID]]
  transfers between devices with their start and end apart: 2 -> 0, of which waited for: 1 -> 0; matrix products, arithmetic and copies ran while one was open for 0% -> 0% of each run, Pallas kernels for 0% -> 0%
where the time goes in v2:
time: 64.5 us; the launch traced here: 64.1 us
  Pallas kernels  61.8 us (96%)
  local copies, waits for them, and re-layouts  2.3 us (4%)
    pallas_call x1, Pallas kernels, body(): pl.pallas_call(functools.partial(fused_kernel, tm_count, sectors, piece,...  61.8 us
    unnamed x1, local copies, waits for them, and re-layouts  2.3 us

profile of v2, /device:TPU:0, one launch (start us, length us, event | category | flops | bytes accessed | tf_op | source)
XLA Modules:
  0.0 64.1 jit_solution(9287666318607473397)
XLA Ops:
  0.0 61.8 %shard_map.100 = bf16[2048,256]{1,0:T(8,128)(2,1)} custom-call(bf16[512,256]{1,0:T(8,128)(2,1)} %bitcast.7, f32[16,512]{1,0:T(8,128)} %bitcast.8, s32[16,512]{1,0:T(8,128)} %bitcast.9, bf16[8,256]{1,0:T(8,128)(2,1)} %time_ref.1, f32[2,2,256]{2,1,0:T(2,128)} %gain_ref.1, bf16[2,256,768]{2,1,0:T(8,128)(2,1)} %qkv_hbm.1, bf16[2,256,256]{2,1,0:T(8,128)(2,1)} %ow_hbm.1, ...), custom_call_target="tpu_custom_call" | custom-call | tf_op jit(solution)/shard_map/pallas_call | solution.py:416
  61.8 2.3 %copy.12 = bf16[1,32,64,256]{3,2,1,0:T(8,128)(2,1)} copy(bf16[1,32,64,256]{3,2,1,0:T(8,128)(2,1)} %bitcast.5) | data formatting | bytes 2097152

commit v3 on v2

--- a/solution.py
+++ b/solution.py
@@ -118,16 +118,15 @@
     return [pltpu.VMEM(shape, F32)] * 4 + [pltpu.VMEM(shape, BF)]
 
 
-def conv_rows(x_ref, cat_ref, first, count):
-    channels = x_ref.shape[1]
-    centre = x_ref[pl.ds(first, count)]
-    values = centre.astype(F32)
-    column = lax.broadcasted_iota(jnp.int32, values.shape, 0) % GRID
+def widen_row(row, cat_ref, place):
+    channels = row.shape[1]
+    values = row.astype(F32)
+    column = lax.broadcasted_iota(jnp.int32, values.shape, 0)
     left = jnp.where(column == 0, 0.0, pltpu.roll(values, 1, 0)).astype(BF)
-    right = jnp.where(column == GRID - 1, 0.0, pltpu.roll(values, count - 1, 0)).astype(BF)
-    cat_ref[pl.ds(first, count), 0:channels] = left
-    cat_ref[pl.ds(first, count), channels : 2 * channels] = centre
-    cat_ref[pl.ds(first, count), 2 * channels :] = right
+    right = jnp.where(column == GRID - 1, 0.0, pltpu.roll(values, GRID - 1, 0)).astype(BF)
+    cat_ref[place, :, 0:channels] = left
+    cat_ref[place, :, channels : 2 * channels] = row
+    cat_ref[place, :, 2 * channels :] = right
 
 
 def fused_kernel(
@@ -163,6 +162,7 @@
     enc_ref,
     x_ref,
     cat_ref,
+    sum_ref,
     load_sem,
     sector_send,
     sector_recv,
@@ -263,7 +263,7 @@
     def back_copy(c, target, source):
         return pltpu.make_async_remote_copy(
             src_ref=enc_ref.at[c, target],
-            dst_ref=x_ref.at[pl.ds(pl.multiple_of(GRID + source * piece + c * chunk, 16), chunk)],
+            dst_ref=x_ref.at[1 + source * chunks + c],
             send_sem=back_send.at[c, target],
             recv_sem=back_recv.at[c, source],
             device_id={"tm": target},
@@ -273,7 +273,8 @@
     @pl.loop(0, chunks)
     def _(c):
         @pl.loop(0, blocks)
-        def _(b):
+        def _(i):
+            b = lax.rem(i + 1 + lax.div(me, per), blocks)
             step = c * blocks + b
             total = None
             for s in range(sectors):
@@ -284,12 +285,15 @@
                 total = part if total is None else total + part
             send_ref[pl.ds(step * per, per)] = total.astype(BF).reshape(per, chunk, channels)
 
-        @pl.loop(1, tm_count)
-        def _(o):
-            go_copy(c, lax.rem(me + o, tm_count), me).start()
+            @pl.loop(b * per, b * per + per)
+            def _(target):
+                @pl.when(target != me)
+                def _():
+                    go_copy(c, target, me).start()
 
         recv_ref[c, me] = send_ref[c * tm_count + me]
 
+    sum_ref[...] = jnp.zeros_like(sum_ref)
     for load in loads:
         load.wait()
     head_sum = head_matrix(channels)
@@ -316,68 +320,70 @@
         def _(o):
             back_copy(c, lax.rem(me + o, tm_count), me).start()
 
-        here = pl.multiple_of(GRID + me * piece + c * chunk, 16)
-        x_ref[pl.ds(here, chunk)] = enc_ref[c, me]
-
-    @pl.loop(0, chunks)
-    def _(c):
-        @pl.loop(1, tm_count)
-        def _(o):
-            back_copy(c, me, lax.rem(me + tm_count - o, tm_count)).wait_recv()
+        x_ref[1 + me * chunks + c] = enc_ref[c, me]
+
+    height = tm_count * chunks
 
     def edge_copy(way):
         return pltpu.make_async_remote_copy(
-            src_ref=x_ref.at[pl.ds(band if way == 0 else GRID, GRID)],
-            dst_ref=x_ref.at[pl.ds(0 if way == 0 else band + GRID, GRID)],
+            src_ref=x_ref.at[height if way == 0 else 1],
+            dst_ref=x_ref.at[0 if way == 0 else height + 1],
             send_sem=edge_send.at[way],
             recv_sem=edge_recv.at[way],
             device_id={"sector": lax.rem(sector + (1 if way == 0 else sectors - 1), sectors)},
             device_id_type=pl.DeviceIdType.MESH,
         )
 
-    blank = jnp.zeros((GRID, channels), BF)
-
-    @pl.when(sector < sectors - 1)
-    def _():
-        edge_copy(0).start()
-
-    @pl.when(sector > 0)
-    def _():
-        edge_copy(1).start()
-
-    @pl.when(sector == 0)
-    def _():
-        x_ref[0:GRID] = blank
-
-    @pl.when(sector == sectors - 1)
-    def _():
-        x_ref[band + GRID : band + 2 * GRID] = blank
-
-    tall = math.gcd(band, 8 * GRID)
-
-    @pl.loop(0, band // tall)
-    def _(i):
-        conv_rows(x_ref, cat_ref, pl.multiple_of(GRID + i * tall, GRID), tall)
+    def add_halo(way):
+        widen_row(x_ref[0 if way == 0 else height + 1], cat_ref, 0)
+        row = 1 if way == 0 else height
+        sum_ref[row] = sum_ref[row] + jnp.dot(
+            cat_ref[0], conv_ref[0 if way == 0 else 2], preferred_element_type=F32
+        )
+
+    for c in range(chunks):
+        if c == chunks - 1:
+
+            @pl.when(sector < sectors - 1)
+            def _():
+                edge_copy(1).wait_recv()
+                add_halo(1)
+
+        @pl.loop(1, tm_count)
+        def _(o):
+            back_copy(c, me, lax.rem(me + tm_count - o, tm_count)).wait_recv()
+
+        if c == 0:
+
+            @pl.when(sector > 0)
+            def _():
+                edge_copy(1).start()
+
+        if c == chunks - 1:
+
+            @pl.when(sector < sectors - 1)
+            def _():
+                edge_copy(0).start()
+
+        for j in range(tm_count):
+            widen_row(x_ref[1 + j * chunks + c], cat_ref, j)
+        wide = cat_ref[...].reshape(tm_count * GRID, 3 * channels)
+        for r in range(3):
+            part = jnp.dot(wide, conv_ref[r], preferred_element_type=F32)
+            part = part.reshape(tm_count, GRID, channels)
+            for j in range(tm_count):
+                row = 2 + j * chunks + c - r
+                extra = part[j]
+                if r == 1:
+                    extra = extra + x_ref[row].astype(F32)
+                sum_ref[row] = sum_ref[row] + extra
 
     @pl.when(sector > 0)
     def _():
         edge_copy(0).wait_recv()
-
-    @pl.when(sector < sectors - 1)
-    def _():
-        edge_copy(1).wait_recv()
-
-    conv_rows(x_ref, cat_ref, 0, GRID)
-    conv_rows(x_ref, cat_ref, band + GRID, GRID)
-
-    @pl.loop(0, band // tall)
-    def _(i):
-        first = pl.multiple_of(i * tall, GRID)
-        total = x_ref[pl.ds(pl.multiple_of(first + GRID, GRID), tall)].astype(F32)
-        for r in range(3):
-            strip = cat_ref[pl.ds(pl.multiple_of(first + r * GRID, GRID), tall)]
-            total = total + jnp.dot(strip, conv_ref[r], preferred_element_type=F32)
-        result_ref[pl.ds(first, tall)] = total.astype(BF)
+        add_halo(0)
+
+    result_ref[...] = sum_ref[1 : height + 1].reshape(height * GRID, channels).astype(BF)
 
     @pl.when(sector < sectors - 1)
     def _():
@@ -405,7 +411,7 @@
     bins = cell_ids.shape[1]
     band = GRID * GRID // sectors
     piece = band // tm_count
-    chunk = math.gcd(64, piece)
+    chunk = GRID
     chunks = piece // chunk
     rows = math.gcd(256, tm_count * chunk)
     conv_flat = conv_weight.reshape(3, 3 * channels, channels)
@@ -434,8 +440,9 @@
             pltpu.VMEM((chunks * tm_count, chunk, channels), BF),
             pltpu.VMEM((chunks, tm_count, chunk, channels), BF),
             pltpu.VMEM((chunks, tm_count, chunk, channels), BF),
-            pltpu.VMEM((band + 2 * GRID, channels), BF),
-            pltpu.VMEM((band + 2 * GRID, 3 * channels), BF),
+            pltpu.VMEM((band // GRID + 2, GRID, channels), BF),
+            pltpu.VMEM((tm_count, GRID, 3 * channels), BF),
+            pltpu.VMEM((band // GRID + 2, GRID, channels), F32),
             dma((5,)),
             dma((far, 3)),
             dma((far, 3)),

time: 64.5 us -> 60.5 us (0.938)
  Pallas kernels: 61.8 us -> 57.8 us
    pallas_call x1, Pallas kernels: 61.8 us -> 57.8 us  [body(): pl.pallas_call(functools.partial(fused_kernel, tm_count, sectors, piece,...]
where the time goes in v3:
time: 60.5 us; the launch traced here: 60.1 us
  Pallas kernels  57.8 us (96%)
  local copies, waits for them, and re-layouts  2.3 us (4%)
    pallas_call x1, Pallas kernels, body(): pl.pallas_call(functools.partial(fused_kernel, tm_count, sectors, piece,...  57.8 us
    unnamed x1, local copies, waits for them, and re-layouts  2.3 us

profile of v3, /device:TPU:0, one launch (start us, length us, event | category | flops | bytes accessed | tf_op | source)
XLA Modules:
  0.0 60.1 jit_solution(1759292656203269435)
XLA Ops:
  0.0 57.8 %shard_map.100 = bf16[2048,256]{1,0:T(8,128)(2,1)} custom-call(bf16[512,256]{1,0:T(8,128)(2,1)} %bitcast.7, f32[16,512]{1,0:T(8,128)} %bitcast.8, s32[16,512]{1,0:T(8,128)} %bitcast.9, bf16[8,256]{1,0:T(8,128)(2,1)} %time_ref.1, f32[2,2,256]{2,1,0:T(2,128)} %gain_ref.1, bf16[2,256,768]{2,1,0:T(8,128)(2,1)} %qkv_hbm.1, bf16[2,256,256]{2,1,0:T(8,128)(2,1)} %ow_hbm.1, ...), custom_call_target="tpu_custom_call" | custom-call | tf_op jit(solution)/shard_map/pallas_call | solution.py:422
  57.8 2.3 %copy.12 = bf16[1,32,64,256]{3,2,1,0:T(8,128)(2,1)} copy(bf16[1,32,64,256]{3,2,1,0:T(8,128)(2,1)} %bitcast.5) | data formatting | bytes 2097152
